TPU v7x, 32 devices: a whole 2x2x4 slice. The times are simulated.
32 devices in a mesh: fsdp: 16 (over z, y, x), replica: 2 (over core).
Axes of the slice: x: 2, y: 2, z: 4, core: 2. Of those that a mesh axis runs over, the one named last changes fastest.
Arguments:
- master: float32 [1024, 8192], P('fsdp', 'replica'), may hold values from -6 to 6
- moment_one: float32 [1024, 8192], P('fsdp', 'replica'), may hold values from -6 to 6
- moment_two: float32 [1024, 8192], P('fsdp', 'replica'), may hold values from 0.5 to 8
- gradients: float32 [2, 1024, 8192], P('replica', 'fsdp'), may hold values from -6 to 6
- new_row: int32 [1024], P('fsdp'), may hold values from 0 to 1023, as said below
Outputs:
- new_master: float32 [1024, 8192], P('fsdp', 'replica')
- new_moment_one: float32 [1024, 8192], P('fsdp', 'replica')
- new_moment_two: float32 [1024, 8192], P('fsdp', 'replica')
- params: bfloat16 [1024, 8192], P('fsdp')
- checksum: float32 [1024], P('fsdp')
Inputs may be any that keep to these rules, and one draw needn't show every extreme that they name: new_row is a permutation; the 64 old rows of one fsdp index send at most 8 rows to the 64 new rows of any one fsdp index, and this most is reached.
All inputs are finite; a program needn't handle non-finite values.
Results may differ from a plain program's by a relative error of at most 0.0025.
Values may be sent and summed in bfloat16 or wider, within the bound.
No kernel may reach another device: no remote copies, remote signals or barrier semaphores. Data moves between devices by JAX's collectives and lax.ppermute only.
A program may use at most 128 MiB of HBM per device.

v0:
```python
import functools
import math

import jax
import jax.numpy as jnp
from jax import lax
from jax.experimental import pallas as pl
from jax.experimental.pallas import tpu as pltpu
from jax.sharding import PartitionSpec as P

LANES = 128
TILE_ROWS = 16
MIB = 1024 * 1024
VMEM_BYTES = 24 * MIB
MOST_SHIFT_PEERS = 16
F32 = jnp.float32
BF16 = jnp.bfloat16


def iota(shape, axis):
    return lax.broadcasted_iota(jnp.int32, shape, axis)


class Sizes:
    def __init__(self, rows, width, peers, copies):
        self.rows, self.width, self.peers, self.copies = rows, width, peers, copies
        self.cap = max(2, 2 * rows // peers)
        self.split = max(1, TILE_ROWS // self.cap)
        self.lines = self.cap * self.split
        self.slots = peers * self.lines
        self.stacked = self.split * rows
        self.body = width // self.split
        self.cb = math.gcd(self.body, 512)
        self.blocks = self.body // self.cb
        self.span = self.split * self.cb
        self.sub = math.gcd(self.cb, 256)
        self.payload = 3 * self.body + LANES


def prepare_kernel(z, rep_ref, origin_ref, new_row_hbm, full_hbm, pick_ref, info_ref, mask_ref, *refs):
    parts, (full_buf, line_buf, sems, line_sem) = refs[: z.copies - 1], refs[z.copies - 1 :]
    step = z.width // z.blocks
    line_copy = pltpu.make_async_copy(new_row_hbm, line_buf, line_sem)
    line_copy.start()
    copies = []
    for k in range(1, z.copies):
        other = lax.rem(rep_ref[0] + k, z.copies)
        for j in range(z.blocks):
            there = pl.ds(pl.multiple_of(other * z.width + j * step, LANES), step)
            copies.append(
                pltpu.make_async_copy(
                    full_hbm.at[:, there], full_buf.at[k - 1, :, pl.ds(j * step, step)], sems.at[k - 1, j]
                )
            )
            copies[-1].start()
    line_copy.wait()
    line = line_buf[...]
    at_row, at_lane = iota((z.rows, z.rows), 0), iota((z.rows, z.rows), 1)
    column = jnp.sum(jnp.where(at_row == at_lane, line.astype(F32), 0.0), axis=1, keepdims=True).astype(jnp.int32)
    target, target_column = line // z.rows, column // z.rows
    earlier = (target_column == target) & (at_row < at_lane)
    rank = jnp.sum(jnp.where(earlier, 1.0, 0.0), axis=0, keepdims=True).astype(jnp.int32)
    shift = lax.rem(target - origin_ref[0] + z.peers, z.peers)
    shift_column = lax.rem(target_column - origin_ref[0] + z.peers, z.peers)
    for h in range(z.split):
        slot = shift * z.lines + h * z.cap + rank
        pick_ref[h] = jnp.where(iota((z.slots, z.rows), 0) == slot, 1.0, 0.0).astype(BF16)
    lane = iota((z.rows, LANES), 1)
    info_ref[...] = jnp.where(lane == 0, (column - target_column * z.rows + 1).astype(F32), 0.0)
    used = jnp.where(lane == shift_column, 1.0, 0.0)
    mask_ref[...] = jnp.max(used, axis=0, keepdims=True).astype(jnp.int32)
    for k in range(1, z.copies):
        for j in range(z.blocks):
            copies[(k - 1) * z.blocks + j].wait()
            at = slice(j * step, (j + 1) * step)
            parts[k - 1][:, at] = full_buf[k - 1, :, at].astype(BF16)


def agree_kernel(left, right, _, out):
    out[...] = jnp.maximum(left[...], right[...])


def choose_kernel(digits, left, right, *outs):
    total = jnp.maximum(left[...], right[...])
    lane = iota(total.shape, 1)
    for digit, out in zip(digits, outs):
        value = jnp.zeros(total.shape, jnp.int32)
        for i, s in enumerate(digit):
            value = value + jnp.where(lane == s, total << i, 0)
        out[0] = jnp.sum(value.astype(F32)).astype(jnp.int32)


def load_kernel(z, rep_ref, info_ref, master_hbm, one_hbm, two_hbm, full_hbm, master, one, two, own, meta_ref, sems):
    base = rep_ref[0] * z.width
    step = z.width // z.blocks
    copies = []
    for j in range(z.blocks):
        at = pl.ds(j * step, step)
        mine = pl.ds(pl.multiple_of(base + j * step, LANES), step)
        copies.append(
            [
                pltpu.make_async_copy(master_hbm.at[:, at], master.at[:, at], sems.at[0, j]),
                pltpu.make_async_copy(one_hbm.at[:, at], one.at[:, at], sems.at[1, j]),
                pltpu.make_async_copy(two_hbm.at[:, at], two.at[:, at], sems.at[2, j]),
                pltpu.make_async_copy(full_hbm.at[:, mine], own.at[:, at], sems.at[3, j]),
            ]
        )
    for i in range(4):
        for j in range(z.blocks):
            copies[j][i].start()
    part = jnp.zeros((z.rows, LANES), F32)
    for j in range(z.blocks):
        copies[j][0].wait()
        for at in range(j * step, (j + 1) * step, LANES):
            weights = 1.0 + ((iota((1, LANES), 1) + (base + at)) % 7).astype(F32) / 7.0
            part = part + master[:, at : at + LANES] * weights
    total = jnp.sum(part, axis=1, keepdims=True) * (1.0 / math.sqrt(z.width * z.copies))
    high = total.astype(BF16).astype(F32)
    middle = (total - high).astype(BF16).astype(F32)
    low = total - high - middle
    lane = iota((z.rows, LANES), 1)
    meta = jnp.where(lane == 1, high, jnp.where(lane == 2, middle, jnp.where(lane == 3, low, info_ref[...])))
    meta_ref[...] = meta.astype(BF16)
    for j in range(z.blocks):
        for i in range(1, 4):
            copies[j][i].wait()


def update_kernel(z, pick_ref, meta_ref, master, one, two, own, *refs):
    received, refs = refs[: z.copies - 1], refs[z.copies :]
    outs, rows_buf = refs[: z.peers], refs[z.peers]
    pick = jnp.concatenate([pick_ref[h] for h in range(z.split)], axis=1)
    for j in range(z.blocks):
        for h in range(z.split):
            for c in range(0, z.cb, z.sub):
                at = j * z.span + h * z.cb + c
                cols = slice(at, at + z.sub)
                summed = own[:, cols]
                for other in received:
                    summed = summed + other[:, cols].astype(F32)
                moved = master[:, cols]
                new_one = 0.9 * one[:, cols] + 0.1 * summed
                new_two = 0.95 * two[:, cols] + 0.05 * summed * summed
                update = new_one * (1.0 / (1.0 - 0.9**10)) / (jnp.sqrt(new_two * (1.0 / (1.0 - 0.95**10))) + 1e-08)
                new_master = moved - 0.05 * (update + 0.1 * moved)
                for i, value in enumerate((new_master, new_one, new_two)):
                    to = i * z.body + j * z.cb + c
                    rows_buf[h * z.rows : (h + 1) * z.rows, to : to + z.sub] = value.astype(BF16)
        for i in range(3):
            at = i * z.body + j * z.cb
            packed = jnp.dot(pick, rows_buf[:, at : at + z.cb], preferred_element_type=F32).astype(BF16)
            for s, out in enumerate(outs):
                out[:, at : at + z.cb] = packed[s * z.lines : (s + 1) * z.lines]
    meta = jnp.concatenate([meta_ref[...]] * z.split, axis=0)
    packed = jnp.dot(pick, meta, preferred_element_type=F32).astype(BF16)
    for s, out in enumerate(outs):
        out[:, 3 * z.body :] = packed[s * z.lines : (s + 1) * z.lines]


def gathered(refs, cols):
    return jnp.concatenate([ref[:, cols] for ref in refs], axis=0)


def placing(z, meta):
    offset = meta[:, :1].astype(F32).astype(jnp.int32)
    piece = lax.rem(iota((z.slots, 1), 0), z.lines) // z.cap
    wanted = jnp.where(offset > 0, offset - 1 + piece * z.rows, -1)
    return jnp.where(iota((z.slots, z.stacked), 1) == wanted, 1.0, 0.0).T.astype(BF16)


def placed(place, values):
    return jnp.dot(place, values, preferred_element_type=F32)


def half_kernel(z, *refs):
    got, (half, place_out) = refs[: z.peers], refs[z.peers :]
    meta = gathered(got, slice(3 * z.body, 3 * z.body + LANES))
    place = placing(z, meta)
    place_out[...] = place
    for j in range(z.blocks):
        rows_out = placed(place, gathered(got, slice(j * z.cb, (j + 1) * z.cb))).astype(BF16)
        for h in range(z.split):
            at = j * z.span + h * z.cb
            half[:, at : at + z.cb] = rows_out[h * z.rows : (h + 1) * z.rows]
    half[:, z.width :] = placed(place, meta)[: z.rows].astype(BF16)


def place_moment(z, i, place, got, out, buf, sems):
    copies = []
    for j in range(z.blocks):
        at = i * z.body + j * z.cb
        rows_out = placed(place, gathered(got, slice(at, at + z.cb)))
        for h in range(z.split):
            col = j * z.span + h * z.cb
            buf[:, col : col + z.cb] = rows_out[h * z.rows : (h + 1) * z.rows]
        cols = pl.ds(j * z.span, z.span)
        copies.append(pltpu.make_async_copy(buf.at[:, cols], out.at[:, cols], sems.at[j]))
        copies[-1].start()
    return copies


def rows_kernel(z, rep_ref, half, place, *refs):
    got, (new_master, params, one_out, two_out, master_buf, one_buf, two_buf, sems) = refs[: z.peers], refs[z.peers :]
    there = pl.ds(pl.multiple_of(rep_ref[0] * z.width, LANES), z.width)
    copies = [pltpu.make_async_copy(half.at[:, : z.width], params.at[:, there], sems.at[0, 0])]
    copies[0].start()
    for j in range(z.blocks):
        at = slice(j * z.span, (j + 1) * z.span)
        master_buf[:, at] = half[:, at].astype(F32)
        cols = pl.ds(j * z.span, z.span)
        copies.append(pltpu.make_async_copy(master_buf.at[:, cols], new_master.at[:, cols], sems.at[1, j]))
        copies[-1].start()
    copies += place_moment(z, 1, place[...], got, one_out, one_buf, sems.at[2])
    copies += place_moment(z, 2, place[...], got, two_out, two_buf, sems.at[3])
    for copy in copies:
        copy.wait()


def finish_kernel(z, rep_ref, half, *refs):
    others, (_, params, checksum, sems) = refs[: z.copies - 1], refs[z.copies - 1 :]
    copies = []
    for k, other in enumerate(others):
        replica = lax.rem(rep_ref[0] + z.copies - (k + 1), z.copies)
        there = pl.ds(pl.multiple_of(replica * z.width, LANES), z.width)
        copies.append(pltpu.make_async_copy(other.at[:, : z.width], params.at[:, there], sems.at[k]))
        copies[-1].start()
    sums = half[:, z.width :].astype(F32)
    for other in others:
        sums = sums + other[:, z.width :].astype(F32)
    lane = iota((z.rows, LANES), 1)
    column = jnp.sum(jnp.where((lane >= 1) & (lane <= 3), sums, 0.0), axis=1, keepdims=True)
    diagonal = iota((z.rows, z.rows), 0) == iota((z.rows, z.rows), 1)
    checksum[...] = jnp.sum(jnp.where(diagonal, column, 0.0), axis=0, keepdims=True)
    for copy in copies:
        copy.wait()


def shifted(value, axis, k, count):
    return lax.ppermute(value, axis, [(i, (i + k) % count) for i in range(count)])


def shift_groups(peers):
    return [[s, s + peers // 2] for s in range(1, peers // 2)]


def agree(used, stride, peers, after, compiler_params):
    vmem = pl.BlockSpec(memory_space=pltpu.VMEM)
    other = lax.ppermute(used, "fsdp", [(i, i ^ stride) for i in range(peers)])
    return pl.pallas_call(
        agree_kernel,
        out_shape=jax.ShapeDtypeStruct((1, LANES), jnp.int32),
        in_specs=[vmem, vmem, pl.BlockSpec(memory_space=pl.ANY)],
        out_specs=vmem,
        compiler_params=compiler_params,
        name="agree",
    )(used, other, after)


def choose_branches(used, after, peers, compiler_params):
    vmem = pl.BlockSpec(memory_space=pltpu.VMEM)
    smem = pl.BlockSpec(memory_space=pltpu.SMEM)
    groups = shift_groups(peers)
    for stride in range(peers // 4):
        if stride and stride & (stride - 1) == 0:
            used = agree(used, stride, peers, after, compiler_params)
    other = lax.ppermute(used, "fsdp", [(i, i ^ (peers // 2)) for i in range(peers)])
    return pl.pallas_call(
        functools.partial(choose_kernel, groups),
        out_shape=[pltpu.SMEM((1,), jnp.int32)] * len(groups),
        in_specs=[vmem, vmem],
        out_specs=[smem] * len(groups),
        compiler_params=compiler_params,
        name="choose",
    )(used, other)


def send_used(peers, group, used, chunks):
    return tuple(
        shifted(chunk, "fsdp", s, peers) if used >> i & 1 else chunk for i, (s, chunk) in enumerate(zip(group, chunks))
    )


def move(z, chunks, chosen):
    if chosen is None:
        got = lax.all_to_all(jnp.concatenate(chunks, axis=0), "fsdp", split_axis=0, concat_axis=0, tiled=True)
        return [got[s * z.lines : (s + 1) * z.lines] for s in range(z.peers)]
    got = list(chunks)
    half = z.peers // 2
    got[half] = shifted(chunks[half], "fsdp", half, z.peers)
    *chosen, got[half] = lax.optimization_barrier((*chosen, got[half]))
    for group, number in zip(shift_groups(z.peers), chosen):
        branches = [
            lambda *values, group=group, used=used: send_used(z.peers, group, used, values)
            for used in range(1 << len(group))
        ]
        for s, value in zip(group, lax.switch(number[0], branches, *[chunks[s] for s in group])):
            got[s] = value
    return got


def shards(master, moment_one, moment_two, gradients, new_row):
    rows, width = master.shape
    peers, copies = lax.axis_size("fsdp"), lax.axis_size("replica")
    z = Sizes(rows, width, peers, copies)
    compiler_params = pltpu.CompilerParams(vmem_limit_bytes=VMEM_BYTES)
    smem = pl.BlockSpec(memory_space=pltpu.SMEM)
    vmem = pl.BlockSpec(memory_space=pltpu.VMEM)
    hbm = pl.BlockSpec(memory_space=pl.ANY)
    dma = pltpu.SemaphoreType.DMA

    replica = lax.axis_index("replica").astype(jnp.int32)
    rep = replica.reshape(1)
    by_shift = 8 <= peers <= MOST_SHIFT_PEERS and peers & (peers - 1) == 0
    origin = (lax.axis_index("fsdp").astype(jnp.int32) if by_shift else jnp.int32(0)).reshape(1)
    state_in = [pltpu.with_memory_space_constraint(x, pltpu.HBM) for x in (master, moment_one, moment_two)]
    full = pltpu.with_memory_space_constraint(gradients[0], pltpu.HBM)

    part = jax.ShapeDtypeStruct((rows, width), BF16)
    pick, info, used, *parts = pl.pallas_call(
        functools.partial(prepare_kernel, z),
        out_shape=[
            jax.ShapeDtypeStruct((z.split, z.slots, rows), BF16),
            jax.ShapeDtypeStruct((rows, LANES), F32),
            jax.ShapeDtypeStruct((1, LANES), jnp.int32),
        ]
        + [part] * (copies - 1),
        in_specs=[smem, smem, hbm, hbm],
        out_specs=[vmem] * (copies + 2),
        scratch_shapes=[
            pltpu.VMEM((copies - 1, rows, width), F32),
            pltpu.VMEM((1, rows), jnp.int32),
            dma((copies - 1, z.blocks)),
            dma,
        ],
        compiler_params=compiler_params,
        cost_estimate=pl.CostEstimate(flops=1 << 30, bytes_accessed=1, transcendentals=0),
        name="prepare",
    )(rep, origin, pltpu.with_memory_space_constraint(new_row.reshape(1, rows), pltpu.HBM), full)
    received = [shifted(value, "replica", k + 1, copies) for k, value in enumerate(parts)]

    loaded = jax.ShapeDtypeStruct((rows, width), F32)
    *state, meta = pl.pallas_call(
        functools.partial(load_kernel, z),
        out_shape=[loaded, loaded, loaded, loaded, jax.ShapeDtypeStruct((rows, LANES), BF16)],
        in_specs=[smem, vmem, hbm, hbm, hbm, hbm],
        out_specs=[vmem] * 5,
        scratch_shapes=[dma((4, z.blocks))],
        compiler_params=compiler_params,
        cost_estimate=pl.CostEstimate(flops=1 << 30, bytes_accessed=1, transcendentals=0),
        name="load",
    )(rep, info, *state_in, full)

    if by_shift:
        used = agree(used, peers // 4, peers, meta, compiler_params)
    chunks = pl.pallas_call(
        functools.partial(update_kernel, z),
        out_shape=[jax.ShapeDtypeStruct((z.lines, z.payload), BF16)] * peers,
        in_specs=[vmem] * (5 + copies) + [hbm],
        out_specs=[vmem] * peers,
        scratch_shapes=[pltpu.VMEM((z.stacked, 3 * z.body), BF16)],
        compiler_params=compiler_params,
        cost_estimate=pl.CostEstimate(
            flops=6 * z.slots * z.stacked * z.body, bytes_accessed=24 * rows * width, transcendentals=rows * width
        ),
        name="update",
    )(pick, meta, *state, *received, used)

    chosen = choose_branches(used, chunks[0], peers, compiler_params) if by_shift else None
    got = move(z, chunks, chosen)

    wide = jax.ShapeDtypeStruct((rows, width), F32)
    full_params = jax.ShapeDtypeStruct((rows, width * copies), BF16)
    half, place = pl.pallas_call(
        functools.partial(half_kernel, z),
        out_shape=(
            jax.ShapeDtypeStruct((rows, width + LANES), BF16),
            jax.ShapeDtypeStruct((z.stacked, z.slots), BF16),
        ),
        in_specs=[vmem] * peers,
        out_specs=(vmem, vmem),
        compiler_params=compiler_params,
        name="place_half",
    )(*got)
    others = [shifted(half, "replica", k, copies) for k in range(1, copies)]

    new_master, params, new_one, new_two = pl.pallas_call(
        functools.partial(rows_kernel, z),
        out_shape=(wide, full_params, wide, wide),
        in_specs=[smem] + [vmem] * (peers + 2),
        out_specs=(hbm, hbm, hbm, hbm),
        scratch_shapes=[pltpu.VMEM((rows, width), F32)] * 3 + [dma((4, z.blocks))],
        compiler_params=compiler_params,
        cost_estimate=pl.CostEstimate(
            flops=4 * z.slots * z.stacked * z.body, bytes_accessed=18 * rows * width, transcendentals=0
        ),
        name="place_rows",
    )(rep, half, place, *got)

    params, checksum = pl.pallas_call(
        functools.partial(finish_kernel, z),
        out_shape=(full_params, jax.ShapeDtypeStruct((1, rows), F32)),
        in_specs=[smem] + [vmem] * copies + [hbm],
        out_specs=(hbm, vmem),
        scratch_shapes=[dma((max(1, copies - 1),))],
        input_output_aliases={copies + 1: 0},
        compiler_params=compiler_params,
        cost_estimate=pl.CostEstimate(flops=0, bytes_accessed=4 * rows * width, transcendentals=0),
        name="finish",
    )(rep, half, *others, params)
    return (new_master, new_one, new_two, params, checksum.reshape(rows))


def solution(mesh):
    return jax.shard_map(
        shards,
        mesh=mesh,
        in_specs=(
            P("fsdp", "replica"),
            P("fsdp", "replica"),
            P("fsdp", "replica"),
            P("replica", "fsdp", None),
            P("fsdp"),
        ),
        out_specs=(
            P("fsdp", "replica"),
            P("fsdp", "replica"),
            P("fsdp", "replica"),
            P("fsdp", None),
            P("fsdp"),
        ),
        check_vma=False,
    )
```

profile of v0, /device:TPU:5, one launch (start us, length us, event | category | flops | bytes accessed | tf_op | source)
XLA Modules:
  0.0 77.9 jit_solution(14136364698724936694)
XLA Ops:
  4.0 2.3 %load.1 = (f32[64,4096]{1,0:T(8,128)S(1)}, f32[64,4096]{1,0:T(8,128)S(1)}, f32[64,4096]{1,0:T(8,128)S(1)}, f32[64,4096]{1,0:T(8,128)S(1)}, bf16[64,128]{1,0:T(8,128)(2,1)S(1)}) custom-call(s32[1]{0:T(128)} %bitcast.rep_ref, f32[64,128]{1,0:T(8,128)S(1)} %get-tuple-element.222.info_ref, f32[64,4096]{1,0:T(8,128)} %master_hbm.1, f32[64,4096]{1,0:T(8,128)} %one_hbm.1, ...), custom_call_target="tpu_custom_call" | custom-call | flops 1073741824 | bytes 1 | tf_op jit(solution)/shard_map/load/pallas_call | solution.py:342
  6.3 1.6 %update.1 = (bf16[16,6272]{1,0:T(8,128)(2,1)S(1)}, bf16[16,6272]{1,0:T(8,128)(2,1)S(1)}, bf16[16,6272]{1,0:T(8,128)(2,1)S(1)}, bf16[16,6272]{1,0:T(8,128)(2,1)S(...) custom-call(bf16[2,256,64]{2,1,0:T(8,128)(2,1)S(1)} %get-tuple-eleme, ...), custom_call_target="tpu_custom_call" | custom-call | flops 402653184 | bytes 6291456 | tf_op jit(solution)/shard_map/update/pallas_call | solution.py:355
  7.9 2.4 %collective-permute-start.33 = (bf16[16,6272]{1,0:T(8,128)(2,1)S(1)}, bf16[16,6272]{1,0:T(8,128)(2,1)S(1)}, u32[]{:S(2)}, u32[]{:S(2)}) collective-permute-start(bf16[16,6272]{1,0:T(8,128)(2,1)S(1)} %get-tuple-element.238), channel_id=1, source_target_pairs={{0,16},{2,18},{4,20},{6,22},{8,24},{10,26},{12,28},{14,30},{16,0},... | collective-permute-start | bytes 602120 | tf_op jit(solution)/shard_map/ppermute | solution.py:239
  11.5 1.5 %collective-permute-done.30.right = s32[1,128]{1,0:T(1,128)S(1)} collective-permute-done((s32[1,128]{1,0:T(1,128)S(1)}, s32[1,128]{1,0:T(1,128)S(1)}, u32[]{:S(2)}, u32[]{:S(2)}) %collective-permute-start.30) | collective-permute-done | bytes 544 | tf_op jit(solution)/shard_map/ppermute | solution.py:248
  13.2 2.5 %collective-permute-done.31.right = s32[1,128]{1,0:T(1,128)S(1)} collective-permute-done((s32[1,128]{1,0:T(1,128)S(1)}, s32[1,128]{1,0:T(1,128)S(1)}, u32[]{:S(2)}, u32[]{:S(2)}) %collective-permute-start.31) | collective-permute-done | bytes 544 | tf_op jit(solution)/shard_map/ppermute | solution.py:248
  15.7 4.3 %collective-permute-done.32.right = s32[1,128]{1,0:T(1,128)S(1)} collective-permute-done((s32[1,128]{1,0:T(1,128)S(1)}, s32[1,128]{1,0:T(1,128)S(1)}, u32[]{:S(2)}, u32[]{:S(2)}) %collective-permute-start.32) | collective-permute-done | bytes 544 | tf_op jit(solution)/shard_map/ppermute | solution.py:266
  20.2 4.7 %conditional.13 = ((bf16[16,6272]{1,0:T(8,128)(2,1)S(1)}, bf16[16,6272]{1,0:T(8,128)(2,1)S(1)})) conditional(s32[]{:T(128)} %bitcast.10, (bf16[16,6272]{1,0:T(8,128)(2,1)S(1)}, bf16[16,6272]{1,0:T(8,128)(2,1)S(1)}) %tuple.127, (bf16[16,6272]{1,0:T(8,128)(2,1)S(1)}, bf16[16,6272]{1,0:T(8,128)(2,1)S(1)}) %tuple.127, ...), branch_computations={%region_24.0_spmd, %region_25.0_spmd, %region_26.0_spmd, %region_2... | conditional | bytes 2408552 | solution.py:296
  21.4 3.4 %collective-permute-done.25 = bf16[16,6272]{1,0:T(8,128)(2,1)S(1)} collective-permute-done((bf16[16,6272]{1,0:T(8,128)(2,1)S(1)}, bf16[16,6272]{1,0:T(8,128)(2,1)S(1)}, u32[]{:S(2)}, u32[]{:S(2)}) %collective-permute-start.25) | collective-permute-done | bytes 200736 | tf_op jit(solution)/shard_map/cond/branch_2_fun/ppermute | solution.py:239
  24.9 7.5 %conditional.12 = ((bf16[16,6272]{1,0:T(8,128)(2,1)S(1)}, bf16[16,6272]{1,0:T(8,128)(2,1)S(1)})) conditional(s32[]{:T(128)} %bitcast.9, (bf16[16,6272]{1,0:T(8,128)(2,1)S(1)}, bf16[16,6272]{1,0:T(8,128)(2,1)S(1)}) %tuple.125, (bf16[16,6272]{1,0:T(8,128)(2,1)S(1)}, bf16[16,6272]{1,0:T(8,128)(2,1)S(1)}) %tuple.125, ...), branch_computations={%region_20.0_spmd, %region_21.0_spmd, %region_22.0_spmd, %region_2... | conditional | bytes 2408552 | solution.py:296
  25.0 7.3 %collective-permute-done.20 = bf16[16,6272]{1,0:T(8,128)(2,1)S(1)} collective-permute-done((bf16[16,6272]{1,0:T(8,128)(2,1)S(1)}, bf16[16,6272]{1,0:T(8,128)(2,1)S(1)}, u32[]{:S(2)}, u32[]{:S(2)}) %collective-permute-start.20) | collective-permute-done | bytes 200736 | tf_op jit(solution)/shard_map/cond/branch_1_fun/ppermute | solution.py:239
  32.4 8.6 %conditional.11 = ((bf16[16,6272]{1,0:T(8,128)(2,1)S(1)}, bf16[16,6272]{1,0:T(8,128)(2,1)S(1)})) conditional(s32[]{:T(128)} %bitcast.8, (bf16[16,6272]{1,0:T(8,128)(2,1)S(1)}, bf16[16,6272]{1,0:T(8,128)(2,1)S(1)}) %tuple.123, (bf16[16,6272]{1,0:T(8,128)(2,1)S(1)}, bf16[16,6272]{1,0:T(8,128)(2,1)S(1)}) %tuple.123, ...), branch_computations={%region_16.0_spmd, %region_17.0_spmd, %region_18.0_spmd, %region_1... | conditional | bytes 2408552 | solution.py:296
  32.4 4.3 %collective-permute-start.17 = (bf16[16,6272]{1,0:T(8,128)(2,1)S(1)}, bf16[16,6272]{1,0:T(8,128)(2,1)S(1)}, u32[]{:S(2)}, u32[]{:S(2)}) collective-permute-start(bf16[16,6272]{1,0:T(8,128)(2,1)S(1)} %get-tuple-element.139), channel_id=1, source_target_pairs={{0,26},{2,28},{4,30},{6,0},{8,2},{10,4},{12,6},{14,8},{16,10},{18,... | collective-permute-start | bytes 602120 | tf_op jit(solution)/shard_map/cond/branch_2_fun/ppermute | solution.py:239
  36.7 4.2 %collective-permute-done.17 = bf16[16,6272]{1,0:T(8,128)(2,1)S(1)} collective-permute-done((bf16[16,6272]{1,0:T(8,128)(2,1)S(1)}, bf16[16,6272]{1,0:T(8,128)(2,1)S(1)}, u32[]{:S(2)}, u32[]{:S(2)}) %collective-permute-start.17) | collective-permute-done | bytes 200736 | tf_op jit(solution)/shard_map/cond/branch_2_fun/ppermute | solution.py:239
  41.0 8.1 %conditional.10 = ((bf16[16,6272]{1,0:T(8,128)(2,1)S(1)}, bf16[16,6272]{1,0:T(8,128)(2,1)S(1)})) conditional(s32[]{:T(128)} %bitcast.7, (bf16[16,6272]{1,0:T(8,128)(2,1)S(1)}, bf16[16,6272]{1,0:T(8,128)(2,1)S(1)}) %tuple.121, (bf16[16,6272]{1,0:T(8,128)(2,1)S(1)}, bf16[16,6272]{1,0:T(8,128)(2,1)S(1)}) %tuple.121, ...), branch_computations={%region_12.0_spmd, %region_13.0_spmd, %region_14.0_spmd, %region_1... | conditional | bytes 2408552 | solution.py:296
  41.0 3.3 %collective-permute-start.13 = (bf16[16,6272]{1,0:T(8,128)(2,1)S(1)}, bf16[16,6272]{1,0:T(8,128)(2,1)S(1)}, u32[]{:S(2)}, u32[]{:S(2)}) collective-permute-start(bf16[16,6272]{1,0:T(8,128)(2,1)S(1)} %get-tuple-element.133), channel_id=1, source_target_pairs={{0,24},{2,26},{4,28},{6,30},{8,0},{10,2},{12,4},{14,6},{16,8},{18,... | collective-permute-start | bytes 602120 | tf_op jit(solution)/shard_map/cond/branch_2_fun/ppermute | solution.py:239
  44.3 4.7 %collective-permute-done.13 = bf16[16,6272]{1,0:T(8,128)(2,1)S(1)} collective-permute-done((bf16[16,6272]{1,0:T(8,128)(2,1)S(1)}, bf16[16,6272]{1,0:T(8,128)(2,1)S(1)}, u32[]{:S(2)}, u32[]{:S(2)}) %collective-permute-start.13) | collective-permute-done | bytes 200736 | tf_op jit(solution)/shard_map/cond/branch_2_fun/ppermute | solution.py:239
  49.1 7.9 %conditional.9 = ((bf16[16,6272]{1,0:T(8,128)(2,1)S(1)}, bf16[16,6272]{1,0:T(8,128)(2,1)S(1)})) conditional(s32[]{:T(128)} %bitcast.6, (bf16[16,6272]{1,0:T(8,128)(2,1)S(1)}, bf16[16,6272]{1,0:T(8,128)(2,1)S(1)}) %tuple.119, (bf16[16,6272]{1,0:T(8,128)(2,1)S(1)}, bf16[16,6272]{1,0:T(8,128)(2,1)S(1)}) %tuple.119, ...), branch_computations={%region_8.0_spmd, %region_9.0_spmd, %region_10.0_spmd, %region_11.... | conditional | bytes 2408552 | solution.py:296
  49.2 7.8 %collective-permute-done.8 = bf16[16,6272]{1,0:T(8,128)(2,1)S(1)} collective-permute-done((bf16[16,6272]{1,0:T(8,128)(2,1)S(1)}, bf16[16,6272]{1,0:T(8,128)(2,1)S(1)}, u32[]{:S(2)}, u32[]{:S(2)}) %collective-permute-start.8) | collective-permute-done | bytes 200736 | tf_op jit(solution)/shard_map/cond/branch_1_fun/ppermute | solution.py:239
  57.0 7.0 %conditional.8 = ((bf16[16,6272]{1,0:T(8,128)(2,1)S(1)}, bf16[16,6272]{1,0:T(8,128)(2,1)S(1)})) conditional(s32[]{:T(128)} %bitcast.5, (bf16[16,6272]{1,0:T(8,128)(2,1)S(1)}, bf16[16,6272]{1,0:T(8,128)(2,1)S(1)}) %tuple.117, (bf16[16,6272]{1,0:T(8,128)(2,1)S(1)}, bf16[16,6272]{1,0:T(8,128)(2,1)S(1)}) %tuple.117, ...), branch_computations={%region_4.0_spmd, %region_5.0_spmd, %region_6.0_spmd, %region_7.0_... | conditional | bytes 2408552 | solution.py:296
  57.0 1.4 %collective-permute-start.5 = (bf16[16,6272]{1,0:T(8,128)(2,1)S(1)}, bf16[16,6272]{1,0:T(8,128)(2,1)S(1)}, u32[]{:S(2)}, u32[]{:S(2)}) collective-permute-start(bf16[16,6272]{1,0:T(8,128)(2,1)S(1)} %get-tuple-element.121), channel_id=1, source_target_pairs={{0,20},{2,22},{4,24},{6,26},{8,28},{10,30},{12,0},{14,2},{16,4},{1... | collective-permute-start | bytes 602120 | tf_op jit(solution)/shard_map/cond/branch_2_fun/ppermute | solution.py:239
  58.5 5.5 %collective-permute-done.5 = bf16[16,6272]{1,0:T(8,128)(2,1)S(1)} collective-permute-done((bf16[16,6272]{1,0:T(8,128)(2,1)S(1)}, bf16[16,6272]{1,0:T(8,128)(2,1)S(1)}, u32[]{:S(2)}, u32[]{:S(2)}) %collective-permute-start.5) | collective-permute-done | bytes 200736 | tf_op jit(solution)/shard_map/cond/branch_2_fun/ppermute | solution.py:239
  64.5 10.0 %collective-permute-start.34 = (bf16[64,4224]{1,0:T(8,128)(2,1)S(1)}, bf16[64,4224]{1,0:T(8,128)(2,1)S(1)}, u32[]{:S(2)}, u32[]{:S(2)}) collective-permute-start(bf16[64,4224]{1,0:T(8,128)(2,1)S(1)} %get-tuple-element.275.half), channel_id=1, source_target_pairs={{0,1},{1,0},{2,3},{3,2},{4,5},{5,4},{6,7},{7,6},{8,9},{9,8},{10,11... | collective-permute-start | bytes 1622024 | tf_op jit(solution)/shard_map/ppermute | solution.py:239
  74.6 2.0 %place_rows.1 = (f32[64,4096]{1,0:T(8,128)}, bf16[64,8192]{1,0:T(8,128)(2,1)}, f32[64,4096]{1,0:T(8,128)}, f32[64,4096]{1,0:T(8,128)}) custom-call(s32[1]{0:T(128)} %bitcast.rep_ref, bf16[64,4224]{1,0:T(8,128)(2,1)S(1)} %get-tuple-element.275.half, bf16[128,256]{1,0:T(8,128)(2,1)S(1)} %get-tuple-element.276.place, ...), custom_call_target="tpu_custom_call" | custom-call | flops 268435456 | bytes 4718592 | tf_op jit(solution)/shard_map/place_rows/pallas_call | solution.py:386
  76.6 1.3 %finish.1 = (bf16[64,8192]{1,0:T(8,128)(2,1)}, f32[1,64]{1,0:T(1,128)}) custom-call(s32[1]{0:T(128)} %bitcast.rep_ref, bf16[64,4224]{1,0:T(8,128)(2,1)S(1)} %get-tuple-element.275.half, bf16[64,4224]{1,0:T(8,128)(2,1)S(1)} %collective-permute-done.34.refs_0_, bf16[64,8192]{1,0:T(8,128)(2,1)} %get-tuple-element.280.refs_1_), custom_call_target="tpu_custom_call", output_to_operand_aliasing={{0}: (3, {})} | custom-call | bytes 1048576 | tf_op jit(solution)/shard_map/finish/pallas_call | solution.py:399
  (25 shorter events, 6.8 us)
Async XLA Ops:
  1.9 4.4 %collective-permute-start.28 = (bf16[64,4096]{1,0:T(8,128)(2,1)S(1)}, bf16[64,4096]{1,0:T(8,128)(2,1)S(1)}, u32[]{:S(2)}, u32[]{:S(2)}) collective-permute-start(bf16[64,4096]{1,0:T(8,128)(2,1)S(1)} %get-tuple-element.228), channel_id=1, source_target_pairs={{0,1},{1,0},{2,3},{3,2},{4,5},{5,4},{6,7},{7,6},{8,9},{9,8},{10,11... | collective-permute-start | bytes 1572872 | tf_op jit(solution)/shard_map/ppermute | solution.py:239
  2.7 3.6 %collective-permute-start.29 = (s32[1,128]{1,0:T(1,128)S(1)}, s32[1,128]{1,0:T(1,128)S(1)}, u32[]{:S(2)}, u32[]{:S(2)}) collective-permute-start(s32[1,128]{1,0:T(1,128)S(1)} %get-tuple-element.229.left), channel_id=1, source_target_pairs={{0,8},{2,10},{4,12},{6,14},{8,0},{10,2},{12,4},{14,6},{16,24},{18,... | collective-permute-start | bytes 1544 | tf_op jit(solution)/shard_map/ppermute | solution.py:248
  7.9 12.2 %collective-permute-start.33 = (bf16[16,6272]{1,0:T(8,128)(2,1)S(1)}, bf16[16,6272]{1,0:T(8,128)(2,1)S(1)}, u32[]{:S(2)}, u32[]{:S(2)}) collective-permute-start(bf16[16,6272]{1,0:T(8,128)(2,1)S(1)} %get-tuple-element.238), channel_id=1, source_target_pairs={{0,16},{2,18},{4,20},{6,22},{8,24},{10,26},{12,28},{14,30},{16,0},... | collective-permute-start | bytes 602120 | tf_op jit(solution)/shard_map/ppermute | solution.py:239
  10.3 2.7 %collective-permute-start.30 = (s32[1,128]{1,0:T(1,128)S(1)}, s32[1,128]{1,0:T(1,128)S(1)}, u32[]{:S(2)}, u32[]{:S(2)}) collective-permute-start(s32[1,128]{1,0:T(1,128)S(1)} %agree.3.refs_1_.left), channel_id=1, source_target_pairs={{0,2},{2,0},{4,6},{6,4},{8,10},{10,8},{12,14},{14,12},{16,18},{18,... | collective-permute-start | bytes 1544 | tf_op jit(solution)/shard_map/ppermute | solution.py:248
  13.0 2.7 %collective-permute-start.31 = (s32[1,128]{1,0:T(1,128)S(1)}, s32[1,128]{1,0:T(1,128)S(1)}, u32[]{:S(2)}, u32[]{:S(2)}) collective-permute-start(s32[1,128]{1,0:T(1,128)S(1)} %agree.4.left), channel_id=1, source_target_pairs={{0,4},{2,6},{4,0},{6,2},{8,12},{10,14},{12,8},{14,10},{16,20},{18,... | collective-permute-start | bytes 1544 | tf_op jit(solution)/shard_map/ppermute | solution.py:248
  15.7 4.3 %collective-permute-start.32 = (s32[1,128]{1,0:T(1,128)S(1)}, s32[1,128]{1,0:T(1,128)S(1)}, u32[]{:S(2)}, u32[]{:S(2)}) collective-permute-start(s32[1,128]{1,0:T(1,128)S(1)} %agree.5.left), channel_id=1, source_target_pairs={{0,16},{2,18},{4,20},{6,22},{8,24},{10,26},{12,28},{14,30},{16,0},... | collective-permute-start | bytes 1544 | tf_op jit(solution)/shard_map/ppermute | solution.py:266
  20.2 4.6 %collective-permute-start.25 = (bf16[16,6272]{1,0:T(8,128)(2,1)S(1)}, bf16[16,6272]{1,0:T(8,128)(2,1)S(1)}, u32[]{:S(2)}, u32[]{:S(2)}) collective-permute-start(bf16[16,6272]{1,0:T(8,128)(2,1)S(1)} %get-tuple-element.151), channel_id=1, source_target_pairs={{0,30},{2,0},{4,2},{6,4},{8,6},{10,8},{12,10},{14,12},{16,14},{18,... | collective-permute-start | bytes 602120 | tf_op jit(solution)/shard_map/cond/branch_2_fun/ppermute | solution.py:239
  24.9 7.4 %collective-permute-start.20 = (bf16[16,6272]{1,0:T(8,128)(2,1)S(1)}, bf16[16,6272]{1,0:T(8,128)(2,1)S(1)}, u32[]{:S(2)}, u32[]{:S(2)}) collective-permute-start(bf16[16,6272]{1,0:T(8,128)(2,1)S(1)} %get-tuple-element.142), channel_id=1, source_target_pairs={{0,12},{2,14},{4,16},{6,18},{8,20},{10,22},{12,24},{14,26},{16,28}... | collective-permute-start | bytes 602120 | tf_op jit(solution)/shard_map/cond/branch_1_fun/ppermute | solution.py:239
  32.4 8.6 %collective-permute-start.17 = (bf16[16,6272]{1,0:T(8,128)(2,1)S(1)}, bf16[16,6272]{1,0:T(8,128)(2,1)S(1)}, u32[]{:S(2)}, u32[]{:S(2)}) collective-permute-start(bf16[16,6272]{1,0:T(8,128)(2,1)S(1)} %get-tuple-element.139), channel_id=1, source_target_pairs={{0,26},{2,28},{4,30},{6,0},{8,2},{10,4},{12,6},{14,8},{16,10},{18,... | collective-permute-start | bytes 602120 | tf_op jit(solution)/shard_map/cond/branch_2_fun/ppermute | solution.py:239
  41.0 8.1 %collective-permute-start.13 = (bf16[16,6272]{1,0:T(8,128)(2,1)S(1)}, bf16[16,6272]{1,0:T(8,128)(2,1)S(1)}, u32[]{:S(2)}, u32[]{:S(2)}) collective-permute-start(bf16[16,6272]{1,0:T(8,128)(2,1)S(1)} %get-tuple-element.133), channel_id=1, source_target_pairs={{0,24},{2,26},{4,28},{6,30},{8,0},{10,2},{12,4},{14,6},{16,8},{18,... | collective-permute-start | bytes 602120 | tf_op jit(solution)/shard_map/cond/branch_2_fun/ppermute | solution.py:239
  49.1 7.9 %collective-permute-start.8 = (bf16[16,6272]{1,0:T(8,128)(2,1)S(1)}, bf16[16,6272]{1,0:T(8,128)(2,1)S(1)}, u32[]{:S(2)}, u32[]{:S(2)}) collective-permute-start(bf16[16,6272]{1,0:T(8,128)(2,1)S(1)} %get-tuple-element.124), channel_id=1, source_target_pairs={{0,6},{2,8},{4,10},{6,12},{8,14},{10,16},{12,18},{14,20},{16,22},{... | collective-permute-start | bytes 602120 | tf_op jit(solution)/shard_map/cond/branch_1_fun/ppermute | solution.py:239
  57.0 7.0 %collective-permute-start.5 = (bf16[16,6272]{1,0:T(8,128)(2,1)S(1)}, bf16[16,6272]{1,0:T(8,128)(2,1)S(1)}, u32[]{:S(2)}, u32[]{:S(2)}) collective-permute-start(bf16[16,6272]{1,0:T(8,128)(2,1)S(1)} %get-tuple-element.121), channel_id=1, source_target_pairs={{0,20},{2,22},{4,24},{6,26},{8,28},{10,30},{12,0},{14,2},{16,4},{1... | collective-permute-start | bytes 602120 | tf_op jit(solution)/shard_map/cond/branch_2_fun/ppermute | solution.py:239
  64.5 12.0 %collective-permute-start.34 = (bf16[64,4224]{1,0:T(8,128)(2,1)S(1)}, bf16[64,4224]{1,0:T(8,128)(2,1)S(1)}, u32[]{:S(2)}, u32[]{:S(2)}) collective-permute-start(bf16[64,4224]{1,0:T(8,128)(2,1)S(1)} %get-tuple-element.275.half), channel_id=1, source_target_pairs={{0,1},{1,0},{2,3},{3,2},{4,5},{5,4},{6,7},{7,6},{8,9},{9,8},{10,11... | collective-permute-start | bytes 1622024 | tf_op jit(solution)/shard_map/ppermute | solution.py:239
where the time goes:
time: 77.2 us; the launch traced here: 77.9 us
  waiting for transfers between devices  41.4 us (54%)
  starting transfers between devices  26.3 us (34%)
  Pallas kernels  9.11 us (12%)
  between operations  0.82 us (1%)
    ppermute x9, waiting for transfers between devices, shifted(): lax.ppermute(value, axis, [(i, (i + k) % count) for i in range(count)])  33.1 us
    ppermute x9, starting transfers between devices, shifted(): lax.ppermute(value, axis, [(i, (i + k) % count) for i in range(count)])  23.5 us
    ppermute x1, waiting for transfers between devices, choose_branches(): lax.ppermute(used, 'fsdp', [(i, i ^ peers // 2) for i in range(peers)])  4.34 us
    ppermute x3, waiting for transfers between devices, agree(): other = lax.ppermute(used, 'fsdp', [(i, i ^ stride) for i in range(peers)])  3.93 us
    ppermute x3, starting transfers between devices, agree(): other = lax.ppermute(used, 'fsdp', [(i, i ^ stride) for i in range(peers)])  2.75 us
    pallas_call x1, Pallas kernels, shards(): pl.pallas_call(functools.partial(load_kernel, z), out_shape=[loaded, load...  2.28 us
    pallas_call x1, Pallas kernels, shards(): pl.pallas_call(functools.partial(rows_kernel, z), out_shape=(wide, full_p...  1.99 us
    pallas_call x1, Pallas kernels, shards(): pl.pallas_call(functools.partial(update_kernel, z), out_shape=[jax.ShapeD...  1.64 us
  transfers between devices with their start and end apart: 13, of which 9 were waited for; matrix products, arithmetic and copies ran while one was open for 0% of the time, Pallas kernels for 6%

commit v1 on v0

--- a/solution.py
+++ b/solution.py
@@ -13,6 +13,8 @@
 MIB = 1024 * 1024
 VMEM_BYTES = 24 * MIB
 MOST_SHIFT_PEERS = 16
+GROUP = 4
+WINDOW = 4
 F32 = jnp.float32
 BF16 = jnp.bfloat16
 
@@ -239,8 +241,15 @@
     return lax.ppermute(value, axis, [(i, (i + k) % count) for i in range(count)])
 
 
+def always_sent(peers):
+    near = [s for s in range(1, peers) if min(s, peers - s) < peers // 4]
+    return [peers // 2] + sorted(near, key=lambda s: (peers // 4 - s) % (peers // 4))
+
+
 def shift_groups(peers):
-    return [[s, s + peers // 2] for s in range(1, peers // 2)]
+    rest = [s for s in range(1, peers) if s not in always_sent(peers)]
+    groups = -(-len(rest) // GROUP)
+    return [rest[g::groups] for g in range(groups)]
 
 
 def agree(used, stride, peers, after, compiler_params):
@@ -256,13 +265,10 @@
     )(used, other, after)
 
 
-def choose_branches(used, after, peers, compiler_params):
+def choose_branches(used, peers, compiler_params):
     vmem = pl.BlockSpec(memory_space=pltpu.VMEM)
     smem = pl.BlockSpec(memory_space=pltpu.SMEM)
     groups = shift_groups(peers)
-    for stride in range(peers // 4):
-        if stride and stride & (stride - 1) == 0:
-            used = agree(used, stride, peers, after, compiler_params)
     other = lax.ppermute(used, "fsdp", [(i, i ^ (peers // 2)) for i in range(peers)])
     return pl.pallas_call(
         functools.partial(choose_kernel, groups),
@@ -280,14 +286,26 @@
     )
 
 
-def move(z, chunks, chosen):
-    if chosen is None:
+def move(z, chunks, used, by_shift, compiler_params):
+    if not by_shift:
         got = lax.all_to_all(jnp.concatenate(chunks, axis=0), "fsdp", split_axis=0, concat_axis=0, tiled=True)
         return [got[s * z.lines : (s + 1) * z.lines] for s in range(z.peers)]
     got = list(chunks)
-    half = z.peers // 2
-    got[half] = shifted(chunks[half], "fsdp", half, z.peers)
-    *chosen, got[half] = lax.optimization_barrier((*chosen, got[half]))
+    always = always_sent(z.peers)
+    for s in always[:WINDOW]:
+        got[s] = shifted(chunks[s], "fsdp", s, z.peers)
+    first, early = always[0], always[2:]
+    for stride, s in zip([stride for stride in range(1, z.peers // 4) if stride & (stride - 1) == 0], early):
+        used = agree(used, stride, z.peers, got[s], compiler_params)
+    for s, after in zip(always[WINDOW:], always):
+        ready = (got[first], used) if after == first else (got[after],)
+        value = lax.optimization_barrier((chunks[s], *ready))[0]
+        got[s] = shifted(value, "fsdp", s, z.peers)
+    chosen = choose_branches(used, z.peers, compiler_params)
+    barred = lax.optimization_barrier((*chosen, *[got[s] for s in always]))
+    chosen = barred[: len(chosen)]
+    for s, value in zip(always, barred[len(chosen) :]):
+        got[s] = value
     for group, number in zip(shift_groups(z.peers), chosen):
         branches = [
             lambda *values, group=group, used=used: send_used(z.peers, group, used, values)
@@ -365,8 +383,7 @@
         name="update",
     )(pick, meta, *state, *received, used)
 
-    chosen = choose_branches(used, chunks[0], peers, compiler_params) if by_shift else None
-    got = move(z, chunks, chosen)
+    got = move(z, chunks, used, by_shift, compiler_params)
 
     wide = jax.ShapeDtypeStruct((rows, width), F32)
     full_params = jax.ShapeDtypeStruct((rows, width * copies), BF16)

time: 77.2 us -> 73.9 us (0.957)
  starting transfers between devices: 26.3 us -> 24.7 us
  waiting for transfers between devices: 41.4 us -> 40.2 us
    ppermute x9 -> x12, starting transfers between devices: 23.5 us -> 17.9 us  [shifted(): lax.ppermute(value, axis, [(i, (i + k) % count) for i in range(count)])]
    ppermute x3, starting transfers between devices: 2.75 us -> 6.74 us  [agree(): other = lax.ppermute(used, 'fsdp', [(i, i ^ stride) for i in range(peers)])]
    ppermute x3, waiting for transfers between devices: 3.93 us -> 1.35 us  [agree(): other = lax.ppermute(used, 'fsdp', [(i, i ^ stride) for i in range(peers)])]
    ppermute x9 -> x12, waiting for transfers between devices: 33.1 us -> 34.9 us  [shifted(): lax.ppermute(value, axis, [(i, (i + k) % count) for i in range(count)])]
  transfers between devices with their start and end apart: 13 -> 16, of which waited for: 9 -> 7; matrix products, arithmetic and copies ran while one was open for 0% -> 0% of each run, Pallas kernels for 6% -> 6%
where the time goes in v1:
time: 73.9 us; the launch traced here: 75 us
  waiting for transfers between devices  40.2 us (54%)
  starting transfers between devices  24.7 us (33%)
  Pallas kernels  9.11 us (12%)
  between operations  0.77 us (1%)
    ppermute x12, waiting for transfers between devices, shifted(): lax.ppermute(value, axis, [(i, (i + k) % count) for i in range(count)])  34.9 us
    ppermute x12, starting transfers between devices, shifted(): lax.ppermute(value, axis, [(i, (i + k) % count) for i in range(count)])  17.9 us
    ppermute x3, starting transfers between devices, agree(): other = lax.ppermute(used, 'fsdp', [(i, i ^ stride) for i in range(peers)])  6.74 us
    ppermute x1, waiting for transfers between devices, choose_branches(): lax.ppermute(used, 'fsdp', [(i, i ^ peers // 2) for i in range(peers)])  3.98 us
    pallas_call x1, Pallas kernels, shards(): pl.pallas_call(functools.partial(load_kernel, z), out_shape=[loaded, load...  2.28 us
    pallas_call x1, Pallas kernels, shards(): pl.pallas_call(functools.partial(rows_kernel, z), out_shape=(wide, full_p...  1.98 us
    pallas_call x1, Pallas kernels, shards(): pl.pallas_call(functools.partial(update_kernel, z), out_shape=[jax.ShapeD...  1.65 us
  transfers between devices with their start and end apart: 16, of which 7 were waited for; matrix products, arithmetic and copies ran while one was open for 0% of the time, Pallas kernels for 6%

profile of v1, /device:TPU:5, one launch (start us, length us, event | category | flops | bytes accessed | tf_op | source)
XLA Modules:
  0.0 75.0 jit_solution(3491274288986489107)
XLA Ops:
  0.6 1.3 %prepare.1 = (bf16[2,256,64]{2,1,0:T(8,128)(2,1)S(1)}, f32[64,128]{1,0:T(8,128)S(1)}, s32[1,128]{1,0:T(1,128)S(1)}, bf16[64,4096]{1,0:T(8,128)(2,1)S(1)}) custom-call(s32[1]{0:T(128)} %bitcast.rep_ref, s32[1]{0:T(128)} %bitcast.1.origin_ref, s32[1,64]{1,0:T(1,128)} %bitcast.9, f32[64,8192]{1,0:T(8,128)} %bitcast.7), custom_call_target="tpu_custom_call" | custom-call | flops 1073741824 | bytes 1 | tf_op jit(solution)/shard_map/prepare/pallas_call | solution.py:337
  1.9 0.7 collective-permute-start.64
  2.7 1.3 %collective-permute-start.65 = (s32[1,128]{1,0:T(1,128)S(1)}, s32[1,128]{1,0:T(1,128)S(1)}, u32[]{:S(2)}, u32[]{:S(2)}) collective-permute-start(s32[1,128]{1,0:T(1,128)S(1)} %get-tuple-element.444.left), channel_id=1, source_target_pairs={{0,8},{2,10},{4,12},{6,14},{8,0},{10,2},{12,4},{14,6},{16,24},{18,... | collective-permute-start | bytes 1544 | tf_op jit(solution)/shard_map/ppermute | solution.py:257
  4.0 2.3 %load.1 = (f32[64,4096]{1,0:T(8,128)S(1)}, f32[64,4096]{1,0:T(8,128)S(1)}, f32[64,4096]{1,0:T(8,128)S(1)}, f32[64,4096]{1,0:T(8,128)S(1)}, bf16[64,128]{1,0:T(8,128)(2,1)S(1)}) custom-call(s32[1]{0:T(128)} %bitcast.rep_ref, f32[64,128]{1,0:T(8,128)S(1)} %get-tuple-element.437.info_ref, f32[64,4096]{1,0:T(8,128)} %master_hbm.1, f32[64,4096]{1,0:T(8,128)} %one_hbm.1, ...), custom_call_target="tpu_custom_call" | custom-call | flops 1073741824 | bytes 1 | tf_op jit(solution)/shard_map/load/pallas_call | solution.py:360
  6.3 1.7 %update.1 = (bf16[16,6272]{1,0:T(8,128)(2,1)S(1)}, bf16[16,6272]{1,0:T(8,128)(2,1)S(1)}, bf16[16,6272]{1,0:T(8,128)(2,1)S(1)}, bf16[16,6272]{1,0:T(8,128)(2,1)S(...) custom-call(bf16[2,256,64]{2,1,0:T(8,128)(2,1)S(1)} %get-tuple-eleme, ...), custom_call_target="tpu_custom_call" | custom-call | flops 402653184 | bytes 6291456 | tf_op jit(solution)/shard_map/update/pallas_call | solution.py:373
  7.9 1.2 %collective-permute-start.67 = (bf16[16,6272]{1,0:T(8,128)(2,1)S(1)}, bf16[16,6272]{1,0:T(8,128)(2,1)S(1)}, u32[]{:S(2)}, u32[]{:S(2)}) collective-permute-start(bf16[16,6272]{1,0:T(8,128)(2,1)S(1)} %get-tuple-element.446), channel_id=1, source_target_pairs={{0,30},{2,0},{4,2},{6,4},{8,6},{10,8},{12,10},{14,12},{16,14},{18,... | collective-permute-start | bytes 602120 | tf_op jit(solution)/shard_map/ppermute | solution.py:241
  9.2 2.1 %collective-permute-start.69 = (bf16[16,6272]{1,0:T(8,128)(2,1)S(1)}, bf16[16,6272]{1,0:T(8,128)(2,1)S(1)}, u32[]{:S(2)}, u32[]{:S(2)}) collective-permute-start(bf16[16,6272]{1,0:T(8,128)(2,1)S(1)} %get-tuple-element.447), channel_id=1, source_target_pairs={{0,4},{2,6},{4,8},{6,10},{8,12},{10,14},{12,16},{14,18},{16,20},{1... | collective-permute-start | bytes 602120 | tf_op jit(solution)/shard_map/ppermute | solution.py:241
  11.3 2.3 %collective-permute-start.71 = (bf16[16,6272]{1,0:T(8,128)(2,1)S(1)}, bf16[16,6272]{1,0:T(8,128)(2,1)S(1)}, u32[]{:S(2)}, u32[]{:S(2)}) collective-permute-start(bf16[16,6272]{1,0:T(8,128)(2,1)S(1)} %get-tuple-element.450), channel_id=1, source_target_pairs={{0,16},{2,18},{4,20},{6,22},{8,24},{10,26},{12,28},{14,30},{16,0},... | collective-permute-start | bytes 602120 | tf_op jit(solution)/shard_map/ppermute | solution.py:241
  13.6 3.1 %collective-permute-start.66 = (s32[1,128]{1,0:T(1,128)S(1)}, s32[1,128]{1,0:T(1,128)S(1)}, u32[]{:S(2)}, u32[]{:S(2)}) collective-permute-start(s32[1,128]{1,0:T(1,128)S(1)} %agree.3.refs_1_.left), channel_id=1, source_target_pairs={{0,2},{2,0},{4,6},{6,4},{8,10},{10,8},{12,14},{14,12},{16,18},{18,... | collective-permute-start | bytes 1544 | tf_op jit(solution)/shard_map/ppermute | solution.py:257
  16.7 1.3 %collective-permute-done.66.right = s32[1,128]{1,0:T(1,128)S(1)} collective-permute-done((s32[1,128]{1,0:T(1,128)S(1)}, s32[1,128]{1,0:T(1,128)S(1)}, u32[]{:S(2)}, u32[]{:S(2)}) %collective-permute-start.66) | collective-permute-done | bytes 544 | tf_op jit(solution)/shard_map/ppermute | solution.py:257
  18.1 2.3 %collective-permute-start.68 = (s32[1,128]{1,0:T(1,128)S(1)}, s32[1,128]{1,0:T(1,128)S(1)}, u32[]{:S(2)}, u32[]{:S(2)}) collective-permute-start(s32[1,128]{1,0:T(1,128)S(1)} %agree.4.left), channel_id=1, source_target_pairs={{0,4},{2,6},{4,0},{6,2},{8,12},{10,14},{12,8},{14,10},{16,20},{18,... | collective-permute-start | bytes 1544 | tf_op jit(solution)/shard_map/ppermute | solution.py:257
  20.4 3.3 %collective-permute-start.75 = (bf16[16,6272]{1,0:T(8,128)(2,1)S(1)}, bf16[16,6272]{1,0:T(8,128)(2,1)S(1)}, u32[]{:S(2)}, u32[]{:S(2)}) collective-permute-start(bf16[16,6272]{1,0:T(8,128)(2,1)S(1)} %get-tuple-element.457), channel_id=1, source_target_pairs={{0,26},{2,28},{4,30},{6,0},{8,2},{10,4},{12,6},{14,8},{16,10},{18,... | collective-permute-start | bytes 602120 | tf_op jit(solution)/shard_map/ppermute | solution.py:241
  23.8 7.0 %collective-permute-done.71.refs_8_ = bf16[16,6272]{1,0:T(8,128)(2,1)S(1)} collective-permute-done((bf16[16,6272]{1,0:T(8,128)(2,1)S(1)}, bf16[16,6272]{1,0:T(8,128)(2,1)S(1)}, u32[]{:S(2)}, u32[]{:S(2)}) %collective-permute-start.71) | collective-permute-done | bytes 200736 | tf_op jit(solution)/shard_map/ppermute | solution.py:241
  30.8 4.0 %collective-permute-done.70.right = s32[1,128]{1,0:T(1,128)S(1)} collective-permute-done((s32[1,128]{1,0:T(1,128)S(1)}, s32[1,128]{1,0:T(1,128)S(1)}, u32[]{:S(2)}, u32[]{:S(2)}) %collective-permute-start.70) | collective-permute-done | bytes 544 | tf_op jit(solution)/shard_map/ppermute | solution.py:272
  34.9 2.8 %collective-permute-done.73.refs_14_ = bf16[16,6272]{1,0:T(8,128)(2,1)S(1)} collective-permute-done((bf16[16,6272]{1,0:T(8,128)(2,1)S(1)}, bf16[16,6272]{1,0:T(8,128)(2,1)S(1)}, u32[]{:S(2)}, u32[]{:S(2)}) %collective-permute-start.73) | collective-permute-done | bytes 200736 | tf_op jit(solution)/shard_map/ppermute | solution.py:241
  37.8 21.5 %conditional.3 = ((bf16[16,6272]{1,0:T(8,128)(2,1)S(1)}, bf16[16,6272]{1,0:T(8,128)(2,1)S(1)}, bf16[16,6272]{1,0:T(8,128)(2,1)S(1)}, bf16[16,6272]{1,0:T(8,128)(2,1)S(1)})) conditional(s32[]{:T(128)} %bitcast.5, (bf16[16,6272]{1,0:T(8,128)(2,1)S(1)}, bf16[16,6272]{1,0:T(8,128)(2,1)S(1)}, ...), branch_computations={%region_16.0_spmd, %region_17.0_spmd, %region_18.0_spmd, %region_1... | conditional | bytes 4817096 | solution.py:314
  37.8 7.6 %collective-permute-start.35 = (bf16[16,6272]{1,0:T(8,128)(2,1)S(1)}, bf16[16,6272]{1,0:T(8,128)(2,1)S(1)}, u32[]{:S(2)}, u32[]{:S(2)}) collective-permute-start(bf16[16,6272]{1,0:T(8,128)(2,1)S(1)} %get-tuple-element.325), channel_id=1, source_target_pairs={{0,14},{2,16},{4,18},{6,20},{8,22},{10,24},{12,26},{14,28},{16,30}... | collective-permute-start | bytes 602120 | tf_op jit(solution)/shard_map/cond/branch_3_fun/ppermute | solution.py:241
  45.4 1.0 %collective-permute-done.34 = bf16[16,6272]{1,0:T(8,128)(2,1)S(1)} collective-permute-done((bf16[16,6272]{1,0:T(8,128)(2,1)S(1)}, bf16[16,6272]{1,0:T(8,128)(2,1)S(1)}, u32[]{:S(2)}, u32[]{:S(2)}) %collective-permute-start.34) | collective-permute-done | bytes 200736 | tf_op jit(solution)/shard_map/cond/branch_3_fun/ppermute | solution.py:241
  46.4 12.8 %collective-permute-done.35 = bf16[16,6272]{1,0:T(8,128)(2,1)S(1)} collective-permute-done((bf16[16,6272]{1,0:T(8,128)(2,1)S(1)}, bf16[16,6272]{1,0:T(8,128)(2,1)S(1)}, u32[]{:S(2)}, u32[]{:S(2)}) %collective-permute-start.35) | collective-permute-done | bytes 200736 | tf_op jit(solution)/shard_map/cond/branch_3_fun/ppermute | solution.py:241
  59.2 11.4 %conditional.2 = ((bf16[16,6272]{1,0:T(8,128)(2,1)S(1)}, bf16[16,6272]{1,0:T(8,128)(2,1)S(1)}, bf16[16,6272]{1,0:T(8,128)(2,1)S(1)}, bf16[16,6272]{1,0:T(8,128)(2,1)S(1)})) conditional(s32[]{:T(128)} %bitcast.4, (bf16[16,6272]{1,0:T(8,128)(2,1)S(1)}, bf16[16,6272]{1,0:T(8,128)(2,1)S(1)}, ...), branch_computations={%region_0.0_spmd, %region_1.0_spmd, %region_2.0_spmd, %region_3.0_... | conditional | bytes 4817096 | solution.py:314
  59.3 11.2 %collective-permute-done.4 = bf16[16,6272]{1,0:T(8,128)(2,1)S(1)} collective-permute-done((bf16[16,6272]{1,0:T(8,128)(2,1)S(1)}, bf16[16,6272]{1,0:T(8,128)(2,1)S(1)}, u32[]{:S(2)}, u32[]{:S(2)}) %collective-permute-start.4) | collective-permute-done | bytes 200736 | tf_op jit(solution)/shard_map/cond/branch_4_fun/ppermute | solution.py:241
  71.1 0.6 collective-permute-start.76
  71.6 2.0 %place_rows.1 = (f32[64,4096]{1,0:T(8,128)}, bf16[64,8192]{1,0:T(8,128)(2,1)}, f32[64,4096]{1,0:T(8,128)}, f32[64,4096]{1,0:T(8,128)}) custom-call(s32[1]{0:T(128)} %bitcast.rep_ref, bf16[64,4224]{1,0:T(8,128)(2,1)S(1)} %get-tuple-element.483.half, bf16[128,256]{1,0:T(8,128)(2,1)S(1)} %get-tuple-element.484.place, ...), custom_call_target="tpu_custom_call" | custom-call | flops 268435456 | bytes 4718592 | tf_op jit(solution)/shard_map/place_rows/pallas_call | solution.py:403
  73.6 1.3 %finish.1 = (bf16[64,8192]{1,0:T(8,128)(2,1)}, f32[1,64]{1,0:T(1,128)}) custom-call(s32[1]{0:T(128)} %bitcast.rep_ref, bf16[64,4224]{1,0:T(8,128)(2,1)S(1)} %get-tuple-element.483.half, bf16[64,4224]{1,0:T(8,128)(2,1)S(1)} %collective-permute-done.76.refs_0_, bf16[64,8192]{1,0:T(8,128)(2,1)} %get-tuple-element.488.refs_1_), custom_call_target="tpu_custom_call", output_to_operand_aliasing={{0}: (3, {})} | custom-call | bytes 1048576 | tf_op jit(solution)/shard_map/finish/pallas_call | solution.py:416
  (23 shorter events, 0.8 us)
Async XLA Ops:
  1.9 4.4 %collective-permute-start.64 = (bf16[64,4096]{1,0:T(8,128)(2,1)S(1)}, bf16[64,4096]{1,0:T(8,128)(2,1)S(1)}, u32[]{:S(2)}, u32[]{:S(2)}) collective-permute-start(bf16[64,4096]{1,0:T(8,128)(2,1)S(1)} %get-tuple-element.443), channel_id=1, source_target_pairs={{0,1},{1,0},{2,3},{3,2},{4,5},{5,4},{6,7},{7,6},{8,9},{9,8},{10,11... | collective-permute-start | bytes 1572872 | tf_op jit(solution)/shard_map/ppermute | solution.py:241
  2.7 3.6 %collective-permute-start.65 = (s32[1,128]{1,0:T(1,128)S(1)}, s32[1,128]{1,0:T(1,128)S(1)}, u32[]{:S(2)}, u32[]{:S(2)}) collective-permute-start(s32[1,128]{1,0:T(1,128)S(1)} %get-tuple-element.444.left), channel_id=1, source_target_pairs={{0,8},{2,10},{4,12},{6,14},{8,0},{10,2},{12,4},{14,6},{16,24},{18,... | collective-permute-start | bytes 1544 | tf_op jit(solution)/shard_map/ppermute | solution.py:257
  7.9 10.2 %collective-permute-start.67 = (bf16[16,6272]{1,0:T(8,128)(2,1)S(1)}, bf16[16,6272]{1,0:T(8,128)(2,1)S(1)}, u32[]{:S(2)}, u32[]{:S(2)}) collective-permute-start(bf16[16,6272]{1,0:T(8,128)(2,1)S(1)} %get-tuple-element.446), channel_id=1, source_target_pairs={{0,30},{2,0},{4,2},{6,4},{8,6},{10,8},{12,10},{14,12},{16,14},{18,... | collective-permute-start | bytes 602120 | tf_op jit(solution)/shard_map/ppermute | solution.py:241
  9.1 14.6 %collective-permute-start.72 = (bf16[16,6272]{1,0:T(8,128)(2,1)S(1)}, bf16[16,6272]{1,0:T(8,128)(2,1)S(1)}, u32[]{:S(2)}, u32[]{:S(2)}) collective-permute-start(bf16[16,6272]{1,0:T(8,128)(2,1)S(1)} %get-tuple-element.451), channel_id=1, source_target_pairs={{0,6},{2,8},{4,10},{6,12},{8,14},{10,16},{12,18},{14,20},{16,22},{... | collective-permute-start | bytes 602120 | tf_op jit(solution)/shard_map/ppermute | solution.py:241
  9.2 14.5 %collective-permute-start.69 = (bf16[16,6272]{1,0:T(8,128)(2,1)S(1)}, bf16[16,6272]{1,0:T(8,128)(2,1)S(1)}, u32[]{:S(2)}, u32[]{:S(2)}) collective-permute-start(bf16[16,6272]{1,0:T(8,128)(2,1)S(1)} %get-tuple-element.447), channel_id=1, source_target_pairs={{0,4},{2,6},{4,8},{6,10},{8,12},{10,14},{12,16},{14,18},{16,20},{1... | collective-permute-start | bytes 602120 | tf_op jit(solution)/shard_map/ppermute | solution.py:241
  11.3 19.5 %collective-permute-start.71 = (bf16[16,6272]{1,0:T(8,128)(2,1)S(1)}, bf16[16,6272]{1,0:T(8,128)(2,1)S(1)}, u32[]{:S(2)}, u32[]{:S(2)}) collective-permute-start(bf16[16,6272]{1,0:T(8,128)(2,1)S(1)} %get-tuple-element.450), channel_id=1, source_target_pairs={{0,16},{2,18},{4,20},{6,22},{8,24},{10,26},{12,28},{14,30},{16,0},... | collective-permute-start | bytes 602120 | tf_op jit(solution)/shard_map/ppermute | solution.py:241
  13.6 4.5 %collective-permute-start.66 = (s32[1,128]{1,0:T(1,128)S(1)}, s32[1,128]{1,0:T(1,128)S(1)}, u32[]{:S(2)}, u32[]{:S(2)}) collective-permute-start(s32[1,128]{1,0:T(1,128)S(1)} %agree.3.refs_1_.left), channel_id=1, source_target_pairs={{0,2},{2,0},{4,6},{6,4},{8,10},{10,8},{12,14},{14,12},{16,18},{18,... | collective-permute-start | bytes 1544 | tf_op jit(solution)/shard_map/ppermute | solution.py:257
  18.1 5.6 %collective-permute-start.68 = (s32[1,128]{1,0:T(1,128)S(1)}, s32[1,128]{1,0:T(1,128)S(1)}, u32[]{:S(2)}, u32[]{:S(2)}) collective-permute-start(s32[1,128]{1,0:T(1,128)S(1)} %agree.4.left), channel_id=1, source_target_pairs={{0,4},{2,6},{4,0},{6,2},{8,12},{10,14},{12,8},{14,10},{16,20},{18,... | collective-permute-start | bytes 1544 | tf_op jit(solution)/shard_map/ppermute | solution.py:257
  20.4 14.5 %collective-permute-start.75 = (bf16[16,6272]{1,0:T(8,128)(2,1)S(1)}, bf16[16,6272]{1,0:T(8,128)(2,1)S(1)}, u32[]{:S(2)}, u32[]{:S(2)}) collective-permute-start(bf16[16,6272]{1,0:T(8,128)(2,1)S(1)} %get-tuple-element.457), channel_id=1, source_target_pairs={{0,26},{2,28},{4,30},{6,0},{8,2},{10,4},{12,6},{14,8},{16,10},{18,... | collective-permute-start | bytes 602120 | tf_op jit(solution)/shard_map/ppermute | solution.py:241
  23.7 11.2 %collective-permute-start.74 = (bf16[16,6272]{1,0:T(8,128)(2,1)S(1)}, bf16[16,6272]{1,0:T(8,128)(2,1)S(1)}, u32[]{:S(2)}, u32[]{:S(2)}) collective-permute-start(bf16[16,6272]{1,0:T(8,128)(2,1)S(1)} %get-tuple-element.455), channel_id=1, source_target_pairs={{0,2},{2,4},{4,6},{6,8},{8,10},{10,12},{12,14},{14,16},{16,18},{18... | collective-permute-start | bytes 602120 | tf_op jit(solution)/shard_map/ppermute | solution.py:241
  30.8 7.0 %collective-permute-start.73 = (bf16[16,6272]{1,0:T(8,128)(2,1)S(1)}, bf16[16,6272]{1,0:T(8,128)(2,1)S(1)}, u32[]{:S(2)}, u32[]{:S(2)}) collective-permute-start(bf16[16,6272]{1,0:T(8,128)(2,1)S(1)} %get-tuple-element.453), channel_id=1, source_target_pairs={{0,28},{2,30},{4,0},{6,2},{8,4},{10,6},{12,8},{14,10},{16,12},{18,... | collective-permute-start | bytes 602120 | tf_op jit(solution)/shard_map/ppermute | solution.py:241
  30.8 4.0 %collective-permute-start.70 = (s32[1,128]{1,0:T(1,128)S(1)}, s32[1,128]{1,0:T(1,128)S(1)}, u32[]{:S(2)}, u32[]{:S(2)}) collective-permute-start(s32[1,128]{1,0:T(1,128)S(1)} %agree.5.left), channel_id=1, source_target_pairs={{0,16},{2,18},{4,20},{6,22},{8,24},{10,26},{12,28},{14,30},{16,0},... | collective-permute-start | bytes 1544 | tf_op jit(solution)/shard_map/ppermute | solution.py:272
  37.8 8.6 %collective-permute-start.34 = (bf16[16,6272]{1,0:T(8,128)(2,1)S(1)}, bf16[16,6272]{1,0:T(8,128)(2,1)S(1)}, u32[]{:S(2)}, u32[]{:S(2)}) collective-permute-start(bf16[16,6272]{1,0:T(8,128)(2,1)S(1)} %get-tuple-element.324), channel_id=1, source_target_pairs={{0,10},{2,12},{4,14},{6,16},{8,18},{10,20},{12,22},{14,24},{16,26}... | collective-permute-start | bytes 602120 | tf_op jit(solution)/shard_map/cond/branch_3_fun/ppermute | solution.py:241
  37.8 21.4 %collective-permute-start.35 = (bf16[16,6272]{1,0:T(8,128)(2,1)S(1)}, bf16[16,6272]{1,0:T(8,128)(2,1)S(1)}, u32[]{:S(2)}, u32[]{:S(2)}) collective-permute-start(bf16[16,6272]{1,0:T(8,128)(2,1)S(1)} %get-tuple-element.325), channel_id=1, source_target_pairs={{0,14},{2,16},{4,18},{6,20},{8,22},{10,24},{12,26},{14,28},{16,30}... | collective-permute-start | bytes 602120 | tf_op jit(solution)/shard_map/cond/branch_3_fun/ppermute | solution.py:241
  59.3 11.3 %collective-permute-start.4 = (bf16[16,6272]{1,0:T(8,128)(2,1)S(1)}, bf16[16,6272]{1,0:T(8,128)(2,1)S(1)}, u32[]{:S(2)}, u32[]{:S(2)}) collective-permute-start(bf16[16,6272]{1,0:T(8,128)(2,1)S(1)} %get-tuple-element.270), channel_id=1, source_target_pairs={{0,18},{2,20},{4,22},{6,24},{8,26},{10,28},{12,30},{14,0},{16,2},{... | collective-permute-start | bytes 602120 | tf_op jit(solution)/shard_map/cond/branch_4_fun/ppermute | solution.py:241
  71.1 2.5 %collective-permute-start.76 = (bf16[64,4224]{1,0:T(8,128)(2,1)S(1)}, bf16[64,4224]{1,0:T(8,128)(2,1)S(1)}, u32[]{:S(2)}, u32[]{:S(2)}) collective-permute-start(bf16[64,4224]{1,0:T(8,128)(2,1)S(1)} %get-tuple-element.483.half), channel_id=1, source_target_pairs={{0,1},{1,0},{2,3},{3,2},{4,5},{5,4},{6,7},{7,6},{8,9},{9,8},{10,11... | collective-permute-start | bytes 1622024 | tf_op jit(solution)/shard_map/ppermute | solution.py:241
